TPU v7x, 32 devices: a whole 2x2x4 slice. The times are simulated.
32 devices in a mesh: ep: 16 (over z, y, x), dp: 2 (over core).
Axes of the slice: x: 2, y: 2, z: 4, core: 2. Of those that a mesh axis runs over, the one named last changes fastest.
Arguments:
- tokens: bfloat16 [4096, 3584], P(('dp', 'ep')), parts along dimension 0, may hold values from -6 to 6
- routes: int32 [4096, 1], P(('dp', 'ep')), parts along dimension 0, may hold values from 0 to 1; in each aligned block of 128 rows (0 to 127, 128 to 255, ...) at most 72 rows name the same one
- route_weight: float32 [4096, 1], P(('dp', 'ep')), parts along dimension 0, may hold values from 0.1 to 1
- norm_gain: bfloat16 [3584], replicated, may hold values from 0.25 to 1.75
- w_gate: bfloat16 [16, 3584, 128], P('ep'), may hold values from -0.09375 to 0.09375
- w_up: bfloat16 [16, 3584, 128], P('ep'), may hold values from -0.09375 to 0.09375
- w_down: bfloat16 [16, 128, 3584], P('ep'), may hold values from -0.1875 to 0.1875
Outputs:
- mixed: bfloat16 [4096, 3584], P(('dp', 'ep')), parts along dimension 0
There are 2 independent parts, one for each index of `dp`. A program takes and returns all parts, laid end to end along the dimension named above; an argument that names none is the same for every part. Nothing has to cross between parts.
Inputs may be any that keep to these rules, and one draw needn't show every extreme that they name: `routes`: each row names 1 different experts; among the rows of one device at most 72 name any one expert, and in every draw some expert is named by exactly 72 rows of some device.
All inputs are finite; a program needn't handle non-finite values.
Results may differ from a plain program's by a relative error of at most 0.0071.
Values may be sent and summed in bfloat16 or wider, within the bound.
A program may use at most 64 MiB of HBM per device.

v0:
```python
import jax
import jax.numpy as jnp
from jax import lax
from jax.sharding import PartitionSpec as P

FFE = 1024


eps_norm = 1e-06


def normalize(tokens, norm_gain):
    values = tokens.astype(jnp.float32)
    inv_scale = lax.rsqrt(jnp.mean(values * values, axis=-1, keepdims=True) + eps_norm)
    return (values * inv_scale * norm_gain.astype(jnp.float32)).astype(jnp.bfloat16)


def body(tokens, routes, route_weight, norm_gain, w_gate, w_up, w_down):
    peer_count = lax.axis_size("ep")
    tok_rows = tokens.shape[0]
    width = tokens.shape[1]
    top_count = routes.shape[1]
    share_count = FFE // w_gate.shape[2]
    expert_count = peer_count // share_count
    cap_rows = max(2, tok_rows * top_count * 9 // (8 * expert_count))
    normed = normalize(tokens, norm_gain)
    flat_expert = routes.reshape(-1)
    route_total = flat_expert.shape[0]
    one_hot = (flat_expert[:, None] == jnp.arange(expert_count, dtype=jnp.int32)[None, :]).astype(
        jnp.int32
    )
    earlier = jnp.cumsum(one_hot, axis=0) - one_hot
    slot_index = jnp.sum(earlier * one_hot, axis=1)
    position = flat_expert * cap_rows + slot_index
    source = jnp.full((expert_count * cap_rows,), route_total, jnp.int32)
    source = source.at[position].set(jnp.arange(route_total, dtype=jnp.int32))
    padded = jnp.concatenate([normed, jnp.zeros((1, width), jnp.bfloat16)], axis=0)
    per_expert = padded[source // top_count].reshape(expert_count, cap_rows, width)
    outgoing = jnp.repeat(per_expert, share_count, axis=0)
    received = lax.all_to_all(outgoing, "ep", split_axis=0, concat_axis=0, tiled=True)
    flat_rows = received.reshape(-1, width)
    gate_act = jnp.dot(flat_rows, w_gate[0], preferred_element_type=jnp.float32)
    up_act = jnp.dot(flat_rows, w_up[0], preferred_element_type=jnp.float32)
    hidden = (jax.nn.silu(gate_act) * up_act).astype(jnp.bfloat16)
    result = jnp.dot(hidden, w_down[0], preferred_element_type=jnp.float32).astype(jnp.bfloat16)
    returned = lax.all_to_all(
        result.reshape(received.shape), "ep", split_axis=0, concat_axis=0, tiled=True
    )
    combined = jnp.sum(
        returned.reshape(expert_count, share_count, cap_rows, width).astype(jnp.float32), axis=1
    )
    picked_rows = combined.reshape(expert_count * cap_rows, width)[position]
    weighted = picked_rows * route_weight.reshape(-1)[:, None]
    mixed = jnp.sum(weighted.reshape(tok_rows, top_count, width), axis=1)
    return mixed.astype(jnp.bfloat16)


def solution(mesh):
    in_specs = (
        P(("dp", "ep"), None),
        P(("dp", "ep"), None),
        P(("dp", "ep"), None),
        P(),
        P("ep", None, None),
        P("ep", None, None),
        P("ep", None, None),
    )
    out_specs = P(("dp", "ep"), None)
    return jax.shard_map(body, mesh=mesh, in_specs=in_specs, out_specs=out_specs, check_vma=False)
```

profile of v0, /device:TPU:28, one launch (start us, length us, event | category | flops | bytes accessed | tf_op | source)
XLA Modules:
  0.0 411.6 jit_solution(13726978857233474216)
XLA Ops:
  0.0 0.0 copy-start
  0.0 0.8 fusion.15
  0.8 0.2 reduce_window_sum.11
  1.0 0.8 select_reduce_fusion
  1.8 0.7 fusion.16
  2.5 1.0 scatter_custom_fusion
  3.5 0.7 convert_element_type.28
  4.2 1.4 fusion.1
  5.7 1.5 fusion.3
  7.1 0.1 concatenate.3
  7.2 1.2 gather_fusion
  8.4 0.6 broadcast_in_dim.8
  9.0 0.0 copy-start.4
  9.0 185.6 %all_to_all.10 = bf16[16,72,3584]{2,1,0:T(8,128)(2,1)S(1)} all-to-all(bf16[16,72,3584]{2,1,0:T(8,128)(2,1)S(1)} %bitcast.32), channel_id=1, replica_groups=mesh['ep'=16,'dp'=2] {'ep'}, dimensions={0} | all-to-all | bytes 16515072 | tf_op jit(solution)/shard_map/all_to_all | solution.py:40
  194.6 3.2 copy-done.1
  197.8 2.3 fusion.7
  200.1 12.9 %convolution_convert_fusion = bf16[1152,3584]{1,0:T(8,128)(2,1)} fusion(bf16[1152,3584]{1,0:T(8,128)(2,1)} %bitcast.31, bf16[1,128,3584]{2,1,0:T(8,128)(2,1)S(1)} %copy-done, bf16[1,3584,128]{2,1,0:T(8,128)(2,1)S(1)} %copy-done.2, f32[1152,128]{1,0:T(8,128)S(1)} %fusion.7), kind=kOutput, calls=%fused_computation.4 | convolution fusion | flops 2118942720 | bytes 18939904 | tf_op jit(solution)/shard_map/dot_general | solution.py:45
  213.0 7.1 %all-to-all-start.1 = ((bf16[16,72,3584]{2,1,0:T(8,128)(2,1)}), bf16[16,72,3584]{2,1,0:T(8,128)(2,1)}, u32[]{:S(2)}, u32[]{:S(2)}) async-start(bf16[16,72,3584]{2,1,0:T(8,128)(2,1)} %bitcast.29), calls=%async_computation.1 | async-start | bytes 16515072 | tf_op jit(solution)/shard_map/all_to_all | solution.py:46
  220.1 181.7 %all-to-all-done.1 = bf16[16,72,3584]{2,1,0:T(8,128)(2,1)} async-done(((bf16[16,72,3584]{2,1,0:T(8,128)(2,1)}), bf16[16,72,3584]{2,1,0:T(8,128)(2,1)}, u32[]{:S(2)}, u32[]{:S(2)}) %all-to-all-start.1) | async-done | bytes 8257568 | tf_op jit(solution)/shard_map/all_to_all | solution.py:46
  401.9 4.7 %convert_reduce_fusion = f32[2,72,3584]{2,1,0:T(8,128)S(1)} fusion(bf16[16,72,3584]{2,1,0:T(8,128)(2,1)} %all-to-all-done.1), kind=kLoop, calls=%fused_computation.3 | loop fusion | flops 7741440 | bytes 10321920 | tf_op jit(solution)/shard_map/reduce_sum | solution.py:49
  406.5 0.0 copy-start.3
  406.5 2.4 gather_fusion.1
  409.0 0.0 copy-done.3
  409.0 2.6 multiply_convert_fusion
  (10 shorter events, 0.0 us)
Async XLA Ops:
  0.0 200.1 %copy-start = (bf16[1,128,3584]{2,1,0:T(8,128)(2,1)S(1)}, bf16[1,128,3584]{2,1,0:T(8,128)(2,1)}, u32[]{:S(2)}) copy-start(bf16[1,128,3584]{2,1,0:T(8,128)(2,1)} %param.13) | copy-start | bytes 2752516
  9.0 188.8 %copy-start.4 = (bf16[1,3584,128]{2,1,0:T(8,128)(2,1)S(1)}, bf16[1,3584,128]{2,1,0:T(8,128)(2,1)}, u32[]{:S(2)}) copy-start(bf16[1,3584,128]{2,1,0:T(8,128)(2,1)} %param.11) | copy-start | bytes 2752516
  194.6 3.2 copy-start.1
  197.8 2.3 copy-start.2
  213.0 188.8 %all-to-all-start.1 = ((bf16[16,72,3584]{2,1,0:T(8,128)(2,1)}), bf16[16,72,3584]{2,1,0:T(8,128)(2,1)}, u32[]{:S(2)}, u32[]{:S(2)}) async-start(bf16[16,72,3584]{2,1,0:T(8,128)(2,1)} %bitcast.29), calls=%async_computation.1 | async-start | bytes 16515072 | tf_op jit(solution)/shard_map/all_to_all | solution.py:46
  406.5 2.4 copy-start.3
where the time goes:
time: 412 us
  blocking collectives  186 us (45%)
  waiting for transfers between devices  182 us (44%)
  matrix products  15.2 us (4%)
  other arithmetic  13.4 us (3%)
  local copies, waits for them, and re-layouts  8.44 us (2%)
  starting transfers between devices  7.07 us (2%)
    all_to_all x1, blocking collectives, body(): lax.all_to_all(outgoing, 'ep', split_axis=0, concat_axis=0, tiled=True)  186 us
    all_to_all x1, waiting for transfers between devices, body(): lax.all_to_all(result.reshape(received.shape), 'ep', split_axis=0, concat...  182 us
    dot_general x1, matrix products, body(): jnp.dot(hidden, w_down[0], preferred_element_type=jnp.float32)  12.9 us
  transfers between devices with their start and end apart: 1, of which 1 were waited for; matrix products, arithmetic and copies ran while one was open for 0% of the time, Pallas kernels for 0%

commit v1 on v0

v1 whole, which is shorter than its diff:
```python
import functools

import jax
import jax.numpy as jnp
from jax import lax
from jax.experimental import pallas as pl
from jax.experimental.pallas import tpu as pltpu
from jax.sharding import PartitionSpec as P

FFE = 1024
MESH = pl.DeviceIdType.MESH
eps_norm = 1e-06
COL_CHUNKS = 4
DIAG_BY_Y = (True, True, True, False) + (True, True, True, False) * 2


def kernel(
    blocks, slot_rows,
    tok_ref, route_ref, rw_ref, gain_ref, wg_ref, wu_ref, wd_ref, out_ref,
    wgu, wdn, normed, packed, rows_in, hidden, part_own, part_send, part_recv, sum_send, sum_recv,
    local_sem, w_send, w_recv, c_send, c_recv, x_send, x_recv, p_send, p_recv, s_send, s_recv,
):
    toks, width = tok_ref.shape
    units = wg_ref.shape[1]
    me = lax.axis_index("ep")
    dp = lax.axis_index("dp")
    core = lax.rem(dp, 2)
    xb, yb, zb = lax.rem(me, 2), lax.rem(me // 2, 2), lax.rem(me // 4, 2)
    block = me // 8
    inner = lax.rem(me, 8)
    x_dev, y_dev, z_dev = me + 1 - 2 * xb, me + 2 - 4 * yb, me + 4 - 8 * zb
    dp_dev = dp + 1 - 2 * core
    m_own, m_y, m_z, m_d = zb * 2 + yb, zb * 2 + 1 - yb, (1 - zb) * 2 + yb, (1 - zb) * 2 + 1 - yb
    cols_n = width // COL_CHUNKS
    quarter = width // 4
    down_quarter = units // 4
    side = blocks * slot_rows

    def peer(r):
        return lax.rem(block + r, blocks)

    def cols(j):
        return pl.ds(j * cols_n, cols_n)

    def slot(index):
        return pl.ds(pl.multiple_of(index * slot_rows, 16), slot_rows)

    barrier = pltpu.get_barrier_semaphore()
    for other in (x_dev, y_dev, z_dev):
        pl.semaphore_signal(barrier, inc=1, device_id={"ep": other}, device_id_type=MESH)
    pl.semaphore_signal(barrier, inc=1, device_id={"dp": dp_dev}, device_id_type=MESH)
    for r in range(1, blocks):
        pl.semaphore_signal(
            barrier, inc=1, device_id={"ep": peer(r) * 8 + inner}, device_id_type=MESH
        )

    local = [
        pltpu.make_async_copy(wg_ref, wgu.at[m_own, :, pl.ds(0, units)], local_sem.at[0]),
        pltpu.make_async_copy(wu_ref, wgu.at[m_own, :, pl.ds(units, units)], local_sem.at[1]),
        pltpu.make_async_copy(
            wd_ref, wdn.at[pl.ds(pl.multiple_of(m_own * units, units), units), :], local_sem.at[2]
        ),
    ]
    for copy in local:
        copy.start()
    pl.semaphore_wait(barrier, 4 + blocks - 1)

    sent = []

    def remote(src, dst, ss, rs, where):
        return pltpu.make_async_remote_copy(
            src_ref=src, dst_ref=dst, send_sem=ss, recv_sem=rs, device_id=where,
            device_id_type=MESH,
        )

    def send(*args):
        copy = remote(*args)
        copy.start()
        sent.append(copy)

    def own_piece(k):
        if k < 4:
            ref = wu_ref if k % 2 else wg_ref
            first = core * (2 * quarter) + (k // 2) * quarter
            return ref.at[pl.ds(pl.multiple_of(first, 128), quarter), :]
        j, p = divmod(k - 4, 2)
        first = core * (2 * down_quarter) + p * down_quarter
        return wd_ref.at[pl.ds(pl.multiple_of(first, 16), down_quarter), cols(j)]

    def place(k, m, half):
        if k < 4:
            first = half * (2 * quarter) + (k // 2) * quarter
            return wgu.at[
                m, pl.ds(pl.multiple_of(first, 128), quarter), pl.ds((k % 2) * units, units)
            ]
        j, p = divmod(k - 4, 2)
        first = m * units + half * (2 * down_quarter) + p * down_quarter
        return wdn.at[pl.ds(pl.multiple_of(first, 16), down_quarter), cols(j)]

    def direct(k):
        for n, dev in ((0, y_dev), (1, z_dev)):
            send(own_piece(k), place(k, m_own, core), w_send.at[k, n], w_recv.at[k, n], {"ep": dev})

    def arrived(k, n, m, half):
        here = place(k, m, half)
        remote(here, here, w_send.at[k, n], w_recv.at[k, n], {"ep": y_dev}).wait_recv()

    def to_core(k, n, m):
        here = place(k, m, core)
        send(here, here, w_send.at[k, 3 + n], w_recv.at[k, 3 + n], {"dp": dp_dev})

    def relay(k):
        for n, m in ((0, m_y), (1, m_z)):
            arrived(k, n, m, core)
            to_core(k, n, m)
            if DIAG_BY_Y[k] == (n == 1):
                here = place(k, m, core)
                send(
                    here, here, w_send.at[k, 2], w_recv.at[k, 2],
                    {"ep": y_dev if DIAG_BY_Y[k] else z_dev},
                )

    def relay_diag(k):
        arrived(k, 2, m_d, core)
        to_core(k, 2, m_d)

    def from_core(k):
        for n, m in ((0, m_y), (1, m_z), (2, m_d)):
            here = place(k, m, 1 - core)
            remote(here, here, w_send.at[k, 3 + n], w_recv.at[k, 3 + n], {"dp": dp_dev}).wait_recv()

    for k in range(4):
        direct(k)

    total = jnp.zeros((toks, 128), jnp.float32)
    for i in range(width // 128):
        values = tok_ref[:, pl.ds(i * 128, 128)].astype(jnp.float32)
        total = total + values * values
    scale = lax.rsqrt(jnp.sum(total, axis=1, keepdims=True) / width + eps_norm)
    route = route_ref[...]
    later = lax.broadcasted_iota(jnp.int32, (toks, toks), 0)
    sooner = lax.broadcasted_iota(jnp.int32, (toks, toks), 1)
    before = (sooner < later).astype(jnp.float32).astype(jnp.bfloat16)
    rank = jnp.zeros((toks, 1), jnp.float32)
    for e in range(blocks):
        named = (route == e).astype(jnp.float32)
        wide = jnp.broadcast_to(named, (toks, 128)).astype(jnp.bfloat16)
        count = jnp.dot(before, wide, preferred_element_type=jnp.float32)
        rank = rank + named * count[:, :1]
    spot = route * slot_rows + rank.astype(jnp.int32)
    table = (lax.broadcasted_iota(jnp.int32, (toks, side), 1) == spot).astype(jnp.float32)
    table = table.astype(jnp.bfloat16)

    own_slot = slot(xb * blocks + block)
    for j in range(COL_CHUNKS):
        values = tok_ref[:, cols(j)].astype(jnp.float32)
        normed[...] = (values * scale * gain_ref[:, cols(j)].astype(jnp.float32)).astype(
            jnp.bfloat16
        )
        packed[:, cols(j)] = lax.dot_general(
            table, normed[...], (((0,), (0,)), ((), ())), preferred_element_type=jnp.float32
        ).astype(jnp.bfloat16)
        for r in range(1, blocks):
            send(
                packed.at[slot(peer(r)), cols(j)], rows_in.at[own_slot, cols(j)],
                c_send.at[j, r], c_recv.at[j, blocks - r], {"ep": peer(r) * 8 + inner},
            )
        send(
            packed.at[slot(block), cols(j)], rows_in.at[own_slot, cols(j)],
            x_send.at[j, 0], x_recv.at[j, 0], {"ep": x_dev},
        )
        rows_in[own_slot, cols(j)] = packed[slot(block), cols(j)]

    for j in range(COL_CHUNKS):
        relay(j)
        for r in range(1, blocks):
            here = rows_in.at[slot(xb * blocks + peer(r)), cols(j)]
            remote(here, here, c_send.at[j, r], c_recv.at[j, r], {"ep": x_dev}).wait_recv()
            send(here, here, x_send.at[j, r], x_recv.at[j, r], {"ep": x_dev})
        direct(4 + 2 * j)
        direct(5 + 2 * j)
    for k in range(4):
        relay_diag(k)
    relay(4)
    relay(5)

    for j in range(COL_CHUNKS):
        for r in range(blocks):
            here = rows_in.at[slot((1 - xb) * blocks + peer(r)), cols(j)]
            remote(here, here, x_send.at[j, r], x_recv.at[j, r], {"ep": x_dev}).wait_recv()
    for copy in local:
        copy.wait()
    for k in range(4):
        from_core(k)

    for m in range(4):
        acts = jnp.dot(rows_in[...], wgu[m], preferred_element_type=jnp.float32)
        gate, up = acts[:, :units], acts[:, units:]
        hidden[:, pl.ds(m * units, units)] = (gate / (1.0 + jnp.exp(-gate)) * up).astype(
            jnp.bfloat16
        )

    own_side = pl.ds(pl.multiple_of(xb * side, 16), side)
    other_side = pl.ds(pl.multiple_of((1 - xb) * side, 16), side)

    def give_back(j):
        here = part_recv.at[:, cols(j)]
        remote(here, here, p_send.at[j], p_recv.at[j], {"ep": x_dev}).wait_recv()
        sum_send[:, cols(j)] = (
            part_own[:, cols(j)] + part_recv[:, cols(j)].astype(jnp.float32)
        ).astype(jnp.bfloat16)
        for r in range(1, blocks):
            send(
                sum_send.at[slot(peer(r)), cols(j)], sum_recv.at[slot(block), cols(j)],
                s_send.at[j, r], s_recv.at[j, blocks - r], {"ep": peer(r) * 8 + inner},
            )
        sum_recv[slot(block), cols(j)] = sum_send[slot(block), cols(j)]

    for j in range(COL_CHUNKS):
        if j + 1 < COL_CHUNKS:
            relay(6 + 2 * j)
            relay(7 + 2 * j)
        for k in (4 + 2 * j, 5 + 2 * j):
            relay_diag(k)
        for k in (4 + 2 * j, 5 + 2 * j):
            from_core(k)
        part_send[:, cols(j)] = jnp.dot(
            hidden[other_side, :], wdn[:, cols(j)], preferred_element_type=jnp.float32
        ).astype(jnp.bfloat16)
        send(
            part_send.at[:, cols(j)], part_recv.at[:, cols(j)], p_send.at[j], p_recv.at[j],
            {"ep": x_dev},
        )
        part_own[:, cols(j)] = jnp.dot(
            hidden[own_side, :], wdn[:, cols(j)], preferred_element_type=jnp.float32
        )
        if j >= 1:
            give_back(j - 1)
    give_back(COL_CHUNKS - 1)

    factor = rw_ref[...]
    for j in range(COL_CHUNKS):
        for r in range(1, blocks):
            here = sum_recv.at[slot(peer(r)), cols(j)]
            remote(here, here, s_send.at[j, r], s_recv.at[j, r], {"ep": x_dev}).wait_recv()
        out_ref[:, cols(j)] = (
            jnp.dot(table, sum_recv[:, cols(j)], preferred_element_type=jnp.float32) * factor
        ).astype(jnp.bfloat16)
    for copy in sent:
        copy.wait_send()


def body(tokens, routes, route_weight, norm_gain, w_gate, w_up, w_down):
    toks, width = tokens.shape
    units = w_gate.shape[2]
    blocks = lax.axis_size("ep") // (FFE // units)
    cap_rows = max(2, toks * 9 // (8 * blocks))
    slot_rows = -(-cap_rows // 16) * 16
    side = blocks * slot_rows
    vmem = pl.BlockSpec(memory_space=pltpu.VMEM)
    hbm = pl.BlockSpec(memory_space=pl.ANY)
    dma = pltpu.SemaphoreType.DMA
    pieces = 4 + 2 * COL_CHUNKS
    return pl.pallas_call(
        functools.partial(kernel, blocks, slot_rows),
        out_shape=jax.ShapeDtypeStruct((toks, width), jnp.bfloat16),
        in_specs=[vmem] * 4 + [hbm] * 3,
        out_specs=vmem,
        scratch_shapes=[
            pltpu.VMEM((4, width, 2 * units), jnp.bfloat16),
            pltpu.VMEM((4 * units, width), jnp.bfloat16),
            pltpu.VMEM((toks, width // COL_CHUNKS), jnp.bfloat16),
            pltpu.VMEM((side, width), jnp.bfloat16),
            pltpu.VMEM((2 * side, width), jnp.bfloat16),
            pltpu.VMEM((2 * side, 4 * units), jnp.bfloat16),
            pltpu.VMEM((side, width), jnp.float32),
            pltpu.VMEM((side, width), jnp.bfloat16),
            pltpu.VMEM((side, width), jnp.bfloat16),
            pltpu.VMEM((side, width), jnp.bfloat16),
            pltpu.VMEM((side, width), jnp.bfloat16),
            dma((3,)),
            dma((pieces, 6)),
            dma((pieces, 6)),
            dma((COL_CHUNKS, blocks)),
            dma((COL_CHUNKS, blocks)),
            dma((COL_CHUNKS, blocks)),
            dma((COL_CHUNKS, blocks)),
            dma((COL_CHUNKS,)),
            dma((COL_CHUNKS,)),
            dma((COL_CHUNKS, blocks)),
            dma((COL_CHUNKS, blocks)),
        ],
        compiler_params=pltpu.CompilerParams(
            collective_id=0, has_side_effects=True, vmem_limit_bytes=48 * 1024 * 1024
        ),
        cost_estimate=pl.CostEstimate(
            flops=2 * 2 * side * width * 12 * units, bytes_accessed=8 << 20, transcendentals=0
        ),
    )(
        tokens, routes, route_weight, norm_gain.reshape(1, width), w_gate[0], w_up[0], w_down[0]
    )


def solution(mesh):
    in_specs = (
        P(("dp", "ep"), None),
        P(("dp", "ep"), None),
        P(("dp", "ep"), None),
        P(),
        P("ep", None, None),
        P("ep", None, None),
        P("ep", None, None),
    )
    out_specs = P(("dp", "ep"), None)
    return jax.shard_map(body, mesh=mesh, in_specs=in_specs, out_specs=out_specs, check_vma=False)
```

time: 412 us -> 101 us (0.25)
  the two profiles are of different devices: /device:TPU:28 before, /device:TPU:0 now
where the time goes in v1:
time: 101 us; the launch traced here: 100 us
  Pallas kernels  93.1 us (92%)
  local copies, waits for them, and re-layouts  7.12 us (7%)
    pallas_call x1, Pallas kernels, body(): pl.pallas_call(functools.partial(kernel, blocks, slot_rows), out_shape=ja...  93.1 us
    unnamed x15, local copies, waits for them, and re-layouts  6.4 us

profile of v1, /device:TPU:0, one launch (start us, length us, event | category | flops | bytes accessed | tf_op | source)
XLA Modules:
  0.0 100.3 jit_solution(9440077849811490229)
XLA Ops:
  0.0 0.0 copy-start.4
  0.0 0.7 reshape.3.gain_ref
  0.7 0.0 copy-done.4
  0.7 0.0 copy-start.5
  0.7 0.1 copy.8.route_ref
  0.9 0.5 copy-done.5
  1.4 0.1 copy.9.rw_ref
  1.5 0.0 copy-start
  1.5 1.2 %copy-done = bf16[128,3584]{1,0:T(8,128)(2,1)S(1)} copy-done((bf16[128,3584]{1,0:T(8,128)(2,1)S(1)}, bf16[128,3584]{1,0:T(8,128)(2,1)}, u32[]{:S(2)}) %copy-start) | copy-done | bytes 917528
  2.7 0.0 copy-start.1
  2.7 1.2 %copy-done.1 = bf16[1,3584,128]{2,1,0:T(8,128)(2,1)S(1)} copy-done((bf16[1,3584,128]{2,1,0:T(8,128)(2,1)S(1)}, bf16[1,3584,128]{2,1,0:T(8,128)(2,1)}, u32[]{:S(2)}) %copy-start.1) | copy-done | bytes 917528
  3.9 0.0 copy-start.2
  3.9 1.2 %copy-done.2 = bf16[1,3584,128]{2,1,0:T(8,128)(2,1)S(1)} copy-done((bf16[1,3584,128]{2,1,0:T(8,128)(2,1)S(1)}, bf16[1,3584,128]{2,1,0:T(8,128)(2,1)}, u32[]{:S(2)}) %copy-start.2) | copy-done | bytes 917528
  5.0 0.0 copy-start.3
  5.0 1.2 %copy-done.3 = bf16[1,128,3584]{2,1,0:T(8,128)(2,1)S(1)} copy-done((bf16[1,128,3584]{2,1,0:T(8,128)(2,1)S(1)}, bf16[1,128,3584]{2,1,0:T(8,128)(2,1)}, u32[]{:S(2)}) %copy-start.3) | copy-done | bytes 917528
  6.2 93.1 %shard_map.73 = bf16[128,3584]{1,0:T(8,128)(2,1)S(1)} custom-call(bf16[128,3584]{1,0:T(8,128)(2,1)S(1)} %copy-done, s32[128,1]{1,0:T(8,128)S(1)} %copy.8.route_ref, f32[128,1]{1,0:T(8,128)S(1)} %copy.9.rw_ref, bf16[1,3584]{1,0:T(2,128)(2,1)S(1)} %reshape.3.gain_ref, bf16[3584,128]{1,0:T(8,128)(2,1)S(1)} %bitcast.3, bf16[3584,128]{1,0:T(8,128)(2,1)S(1)} %bitcast.4, ...), custom_call_target="tpu_custom_call" | custom-call | flops 3523215360 | bytes 8388608 | tf_op jit(solution)/shard_map/pallas_call | solution.py:264
  99.3 0.9 copy.11
Async XLA Ops:
  0.0 0.7 copy-start.4
  0.7 0.7 copy-start.5
  1.5 1.2 %copy-start = (bf16[128,3584]{1,0:T(8,128)(2,1)S(1)}, bf16[128,3584]{1,0:T(8,128)(2,1)}, u32[]{:S(2)}) copy-start(bf16[128,3584]{1,0:T(8,128)(2,1)} %tok_ref.1) | copy-start | bytes 2752516
  2.7 1.2 %copy-start.1 = (bf16[1,3584,128]{2,1,0:T(8,128)(2,1)S(1)}, bf16[1,3584,128]{2,1,0:T(8,128)(2,1)}, u32[]{:S(2)}) copy-start(bf16[1,3584,128]{2,1,0:T(8,128)(2,1)} %param.11) | copy-start | bytes 2752516
  3.9 1.2 %copy-start.2 = (bf16[1,3584,128]{2,1,0:T(8,128)(2,1)S(1)}, bf16[1,3584,128]{2,1,0:T(8,128)(2,1)}, u32[]{:S(2)}) copy-start(bf16[1,3584,128]{2,1,0:T(8,128)(2,1)} %param.12) | copy-start | bytes 2752516
  5.0 1.2 %copy-start.3 = (bf16[1,128,3584]{2,1,0:T(8,128)(2,1)S(1)}, bf16[1,128,3584]{2,1,0:T(8,128)(2,1)}, u32[]{:S(2)}) copy-start(bf16[1,128,3584]{2,1,0:T(8,128)(2,1)} %param.13) | copy-start | bytes 2752516

commit v2 on v1

v2 whole, which is shorter than its diff:
```python
import functools

import jax
import jax.numpy as jnp
from jax import lax
from jax.experimental import pallas as pl
from jax.experimental.pallas import tpu as pltpu
from jax.sharding import PartitionSpec as P

FFE = 1024
MESH = pl.DeviceIdType.MESH
eps_norm = 1e-06
CHUNKS = (2, 4, 4, 2, 2)
DIAG_BY_Y = (True, True, True, False) + (True, True, True, False, True) * 2


def kernel(
    blocks, half_rows,
    tok_ref, route_ref, rw_ref, gain_ref, wg_ref, wu_ref, wd_ref, out_ref,
    tok_in, wgu, wdn, packed, rows_in, hidden, part_own, part_send, part_recv, sum_send, sum_recv,
    local_sem, w_send, w_recv, c_send, c_recv, x_send, x_recv, p_send, p_recv, s_send, s_recv,
):
    toks, width = tok_ref.shape
    half = width // 2
    slot_rows = 2 * half_rows
    units = wg_ref.shape[1]
    me = lax.axis_index("ep")
    dp = lax.axis_index("dp")
    core = lax.rem(dp, 2)
    xb, yb, zb = lax.rem(me, 2), lax.rem(me // 2, 2), lax.rem(me // 4, 2)
    block = me // 8
    inner = lax.rem(me, 8)
    x_dev, y_dev, z_dev = me + 1 - 2 * xb, me + 2 - 4 * yb, me + 4 - 8 * zb
    dp_dev = dp + 1 - 2 * core
    m_own, m_y, m_z, m_d = zb * 2 + yb, zb * 2 + 1 - yb, (1 - zb) * 2 + yb, (1 - zb) * 2 + 1 - yb
    last = len(CHUNKS) - 1
    quarter = width // 4
    down_rows = units // 2
    side = blocks * slot_rows

    def peer(r):
        return lax.rem(block + r, blocks)

    def cols(j, h=0):
        return pl.ds(h * half + sum(CHUNKS[:j]) * 128, CHUNKS[j] * 128)

    def slot(index):
        return pl.ds(pl.multiple_of(index * slot_rows, 16), slot_rows)

    barrier = pltpu.get_barrier_semaphore()
    for other in (x_dev, y_dev, z_dev):
        pl.semaphore_signal(barrier, inc=1, device_id={"ep": other}, device_id_type=MESH)
    pl.semaphore_signal(barrier, inc=1, device_id={"dp": dp_dev}, device_id_type=MESH)
    for r in range(1, blocks):
        pl.semaphore_signal(
            barrier, inc=1, device_id={"ep": peer(r) * 8 + inner}, device_id_type=MESH
        )

    local = [
        pltpu.make_async_copy(wg_ref, wgu.at[m_own, :, pl.ds(0, units)], local_sem.at[0]),
        pltpu.make_async_copy(wu_ref, wgu.at[m_own, :, pl.ds(units, units)], local_sem.at[1]),
        pltpu.make_async_copy(
            wd_ref, wdn.at[pl.ds(pl.multiple_of(m_own * units, units), units), :], local_sem.at[2]
        ),
    ]
    tok_copy = pltpu.make_async_copy(tok_ref, tok_in, local_sem.at[3])
    tok_copy.start()
    for copy in local:
        copy.start()
    pl.semaphore_wait(barrier, 4 + blocks - 1)

    sent = []

    def remote(src, dst, ss, rs, where):
        return pltpu.make_async_remote_copy(
            src_ref=src, dst_ref=dst, send_sem=ss, recv_sem=rs, device_id=where,
            device_id_type=MESH,
        )

    def send(*args):
        copy = remote(*args)
        copy.start()
        sent.append(copy)

    def own_piece(k):
        if k < 4:
            ref = wu_ref if k % 2 else wg_ref
            first = core * (2 * quarter) + (k // 2) * quarter
            return ref.at[pl.ds(pl.multiple_of(first, 128), quarter), :]
        j, p = divmod(k - 4, 2)
        first = core * down_rows
        return wd_ref.at[pl.ds(pl.multiple_of(first, 16), down_rows), cols(j, p)]

    def place(k, m, part):
        if k < 4:
            first = part * (2 * quarter) + (k // 2) * quarter
            return wgu.at[
                m, pl.ds(pl.multiple_of(first, 128), quarter), pl.ds((k % 2) * units, units)
            ]
        j, p = divmod(k - 4, 2)
        first = m * units + part * down_rows
        return wdn.at[pl.ds(pl.multiple_of(first, 16), down_rows), cols(j, p)]

    def direct(k, n):
        send(
            own_piece(k), place(k, m_own, core), w_send.at[k, n], w_recv.at[k, n],
            {"ep": (y_dev, z_dev)[n]},
        )

    def arrived(k, n, m, part):
        here = place(k, m, part)
        remote(here, here, w_send.at[k, n], w_recv.at[k, n], {"ep": y_dev}).wait_recv()

    def to_core(k, n, m):
        here = place(k, m, core)
        send(here, here, w_send.at[k, 3 + n], w_recv.at[k, 3 + n], {"dp": dp_dev})

    def relay(k, n):
        m = (m_y, m_z)[n]
        arrived(k, n, m, core)
        to_core(k, n, m)
        if DIAG_BY_Y[k] == (n == 1):
            here = place(k, m, core)
            send(
                here, here, w_send.at[k, 2], w_recv.at[k, 2],
                {"ep": y_dev if DIAG_BY_Y[k] else z_dev},
            )

    def relay_diag(k):
        arrived(k, 2, m_d, core)
        to_core(k, 2, m_d)

    def from_core(k, n, m):
        here = place(k, m, 1 - core)
        remote(here, here, w_send.at[k, 3 + n], w_recv.at[k, 3 + n], {"dp": dp_dev}).wait_recv()

    def down(step, j, *rest):
        step(4 + 2 * j, *rest)
        step(5 + 2 * j, *rest)

    for k in (0, 1, 2, 4, 5, 3):
        direct(k, 1)
        direct(k, 0)
    tok_copy.wait()

    def as_column(line):
        down_index = lax.broadcasted_iota(jnp.int32, (toks, toks), 0)
        across = lax.broadcasted_iota(jnp.int32, (toks, toks), 1)
        square = jnp.where(down_index == across, jnp.broadcast_to(line, (toks, toks)), 0.0)
        return jnp.sum(square, axis=1, keepdims=True)

    total = jnp.zeros((toks, 128), jnp.float32)
    for i in range(width // 128):
        values = tok_in[:, pl.ds(i * 128, 128)].astype(jnp.float32)
        total = total + values * values
    scale = lax.rsqrt(jnp.sum(total, axis=1, keepdims=True) / width + eps_norm)
    route = as_column(route_ref[...].astype(jnp.float32)).astype(jnp.int32)
    later = lax.broadcasted_iota(jnp.int32, (toks, toks), 0)
    sooner = lax.broadcasted_iota(jnp.int32, (toks, toks), 1)
    before = (sooner < later).astype(jnp.float32).astype(jnp.bfloat16)
    rank = jnp.zeros((toks, 1), jnp.float32)
    for e in range(blocks):
        named = (route == e).astype(jnp.float32)
        wide = jnp.broadcast_to(named, (toks, 128)).astype(jnp.bfloat16)
        count = jnp.dot(before, wide, preferred_element_type=jnp.float32)
        rank = rank + named * count[:, :1]
    tables = []
    for h in range(2):
        spot = route * slot_rows + h * half_rows + rank.astype(jnp.int32)
        one = (lax.broadcasted_iota(jnp.int32, (toks, side), 1) == spot).astype(jnp.float32)
        tables.append(one.astype(jnp.bfloat16))

    own_slot = slot(xb * blocks + block)
    for j in range(last + 1):
        total = jnp.zeros((side, CHUNKS[j] * 128), jnp.float32)
        for h in range(2):
            values = tok_in[:, cols(j, h)].astype(jnp.float32)
            normed = (values * scale * gain_ref[:, cols(j, h)].astype(jnp.float32)).astype(
                jnp.bfloat16
            )
            total = total + lax.dot_general(
                tables[h], normed, (((0,), (0,)), ((), ())), preferred_element_type=jnp.float32
            )
        packed[:, cols(j)] = total.astype(jnp.bfloat16)
        for r in range(1, blocks):
            send(
                packed.at[slot(peer(r)), cols(j)], rows_in.at[own_slot, cols(j)],
                c_send.at[j, r], c_recv.at[j, blocks - r], {"ep": peer(r) * 8 + inner},
            )
        send(
            packed.at[slot(block), cols(j)], rows_in.at[own_slot, cols(j)],
            x_send.at[j, 0], x_recv.at[j, 0], {"ep": x_dev},
        )
        rows_in[own_slot, cols(j)] = packed[slot(block), cols(j)]

    def relay_rows(j):
        for r in range(1, blocks):
            here = rows_in.at[slot(xb * blocks + peer(r)), cols(j)]
            remote(here, here, c_send.at[j, r], c_recv.at[j, r], {"ep": x_dev}).wait_recv()
            send(here, here, x_send.at[j, r], x_recv.at[j, r], {"ep": x_dev})

    def acts(m):
        low = jnp.dot(rows_in[...], wgu[m, :half, :], preferred_element_type=jnp.float32)
        high = jnp.dot(rows_in[...], wgu[m, half:, :], preferred_element_type=jnp.float32)
        parts = []
        for i in range(2 * blocks):
            first = i * slot_rows
            both = low[first:first + half_rows] + high[first + half_rows:first + slot_rows]
            gate, up = both[:, :units], both[:, units:]
            parts.append(gate / (1.0 + jnp.exp(-gate)) * up)
        hidden[m] = jnp.concatenate(parts, axis=0).astype(jnp.bfloat16)

    relay(0, 0)
    relay(0, 1)
    relay_rows(0)
    relay(1, 0)
    relay(2, 0)
    relay(1, 1)
    relay_rows(1)
    relay_diag(0)
    down(relay, 0, 0)
    relay(3, 0)
    relay(2, 1)
    relay_rows(2)
    relay_diag(1)
    down(relay, 0, 1)
    for j in range(3, last + 1):
        relay_rows(j)
    relay(3, 1)
    down(direct, 1, 0)
    down(direct, 1, 1)
    for j in range(last + 1):
        for r in range(blocks):
            here = rows_in.at[slot((1 - xb) * blocks + peer(r)), cols(j)]
            remote(here, here, x_send.at[j, r], x_recv.at[j, r], {"ep": x_dev}).wait_recv()
    for copy in local:
        copy.wait()
    acts(m_own)
    relay_diag(2)
    for k in range(4):
        from_core(k, 0, m_y)
    acts(m_y)
    down(relay_diag, 0)
    relay_diag(3)
    for j in range(2, last + 1):
        down(direct, j, 0)
        down(direct, j, 1)
    for k in range(4):
        from_core(k, 1, m_z)
    acts(m_z)
    down(relay, 1, 0)
    down(relay, 1, 1)
    for k in range(4):
        from_core(k, 2, m_d)
    acts(m_d)

    own_side = pl.ds(pl.multiple_of(xb * blocks * half_rows, 16), blocks * half_rows)
    other_side = pl.ds(pl.multiple_of((1 - xb) * blocks * half_rows, 16), blocks * half_rows)

    def partial(rows, j):
        ends = []
        for h in range(2):
            total = jnp.zeros((blocks * half_rows, CHUNKS[j] * 128), jnp.float32)
            for m in range(4):
                total = total + jnp.dot(
                    hidden[m, rows, :], wdn[pl.ds(m * units, units), cols(j, h)],
                    preferred_element_type=jnp.float32,
                )
            ends.append(total)
        pieces = []
        for e in range(blocks):
            for h in range(2):
                pieces.append(ends[h][e * half_rows:(e + 1) * half_rows])
        return jnp.concatenate(pieces, axis=0)

    def give_back(j):
        here = part_recv.at[:, cols(j)]
        remote(here, here, p_send.at[j], p_recv.at[j], {"ep": x_dev}).wait_recv()
        sum_send[:, cols(j)] = (
            part_own[:, cols(j)] + part_recv[:, cols(j)].astype(jnp.float32)
        ).astype(jnp.bfloat16)
        for r in range(1, blocks):
            send(
                sum_send.at[slot(peer(r)), cols(j)], sum_recv.at[slot(block), cols(j)],
                s_send.at[j, r], s_recv.at[j, blocks - r], {"ep": peer(r) * 8 + inner},
            )
        sum_recv[slot(block), cols(j)] = sum_send[slot(block), cols(j)]

    for j in range(last + 1):
        for n, m in ((0, m_y), (1, m_z), (2, m_d)):
            down(lambda k: from_core(k, n, m), j)
        part_send[:, cols(j)] = partial(other_side, j).astype(jnp.bfloat16)
        send(
            part_send.at[:, cols(j)], part_recv.at[:, cols(j)], p_send.at[j], p_recv.at[j],
            {"ep": x_dev},
        )
        part_own[:, cols(j)] = partial(own_side, j)
        if j >= 1:
            give_back(j - 1)
        if j < last:
            down(relay_diag, j + 1)
        if j + 1 < last:
            down(relay, j + 2, 0)
            down(relay, j + 2, 1)
    give_back(last)

    factor = as_column(rw_ref[...])
    for j in range(last + 1):
        for r in range(1, blocks):
            here = sum_recv.at[slot(peer(r)), cols(j)]
            remote(here, here, s_send.at[j, r], s_recv.at[j, r], {"ep": x_dev}).wait_recv()
        for h in range(2):
            out_ref[:, cols(j, h)] = (
                jnp.dot(tables[h], sum_recv[:, cols(j)], preferred_element_type=jnp.float32)
                * factor
            ).astype(jnp.bfloat16)
    for copy in sent:
        copy.wait_send()


def body(tokens, routes, route_weight, norm_gain, w_gate, w_up, w_down):
    toks, width = tokens.shape
    units = w_gate.shape[2]
    blocks = lax.axis_size("ep") // (FFE // units)
    cap_rows = max(2, toks * 9 // (8 * blocks))
    half_rows = -(-cap_rows // 8) * 8
    side = blocks * 2 * half_rows
    half = width // 2
    chunks = len(CHUNKS)
    vmem = pl.BlockSpec(memory_space=pltpu.VMEM)
    hbm = pl.BlockSpec(memory_space=pl.ANY)
    dma = pltpu.SemaphoreType.DMA
    pieces = 4 + 2 * chunks
    return pl.pallas_call(
        functools.partial(kernel, blocks, half_rows),
        out_shape=jax.ShapeDtypeStruct((toks, width), jnp.bfloat16),
        in_specs=[hbm] + [vmem] * 3 + [hbm] * 3,
        out_specs=vmem,
        scratch_shapes=[
            pltpu.VMEM((toks, width), jnp.bfloat16),
            pltpu.VMEM((4, width, 2 * units), jnp.bfloat16),
            pltpu.VMEM((4 * units, width), jnp.bfloat16),
            pltpu.VMEM((side, half), jnp.bfloat16),
            pltpu.VMEM((2 * side, half), jnp.bfloat16),
            pltpu.VMEM((4, side, units), jnp.bfloat16),
            pltpu.VMEM((side, half), jnp.float32),
            pltpu.VMEM((side, half), jnp.bfloat16),
            pltpu.VMEM((side, half), jnp.bfloat16),
            pltpu.VMEM((side, half), jnp.bfloat16),
            pltpu.VMEM((side, half), jnp.bfloat16),
            dma((4,)),
            dma((pieces, 6)),
            dma((pieces, 6)),
            dma((chunks, blocks)),
            dma((chunks, blocks)),
            dma((chunks, blocks)),
            dma((chunks, blocks)),
            dma((chunks,)),
            dma((chunks,)),
            dma((chunks, blocks)),
            dma((chunks, blocks)),
        ],
        compiler_params=pltpu.CompilerParams(
            collective_id=0, has_side_effects=True, vmem_limit_bytes=60 * 1024 * 1024
        ),
        cost_estimate=pl.CostEstimate(
            flops=2 * 2 * side * width * 12 * units, bytes_accessed=8 << 20, transcendentals=0
        ),
    )(
        tokens, routes.reshape(1, toks), route_weight.reshape(1, toks), norm_gain.reshape(1, width), w_gate[0], w_up[0], w_down[0]
    )


def solution(mesh):
    in_specs = (
        P(("dp", "ep"), None),
        P(("dp", "ep"), None),
        P(("dp", "ep"), None),
        P(),
        P("ep", None, None),
        P("ep", None, None),
        P("ep", None, None),
    )
    out_specs = P(("dp", "ep"), None)
    return jax.shard_map(body, mesh=mesh, in_specs=in_specs, out_specs=out_specs, check_vma=False)
```

time: 101 us -> 92.7 us (0.918)
  Pallas kernels: 93.1 us -> 88.9 us
  local copies, waits for them, and re-layouts: 7.12 us -> 3.47 us
    pallas_call x1, Pallas kernels: 93.1 us -> 88.9 us  [body(): pl.pallas_call(functools.partial(kernel, blocks, half_rows), out_shape=ja...]
    unnamed x15 -> x3, local copies, waits for them, and re-layouts: 6.4 us -> 2.86 us
where the time goes in v2:
time: 92.7 us; the launch traced here: 92.4 us
  Pallas kernels  88.9 us (96%)
  local copies, waits for them, and re-layouts  3.47 us (4%)
    pallas_call x1, Pallas kernels, body(): pl.pallas_call(functools.partial(kernel, blocks, half_rows), out_shape=ja...  88.9 us
    unnamed x3, local copies, waits for them, and re-layouts  2.86 us

profile of v2, /device:TPU:0, one launch (start us, length us, event | category | flops | bytes accessed | tf_op | source)
XLA Modules:
  0.0 92.4 jit_solution(3315300213235333683)
XLA Ops:
  0.0 0.0 copy-start
  0.0 0.7 copy-done
  0.7 0.6 reshape.11.gain_ref
  1.3 88.9 %shard_map.73 = bf16[128,3584]{1,0:T(8,128)(2,1)} custom-call(bf16[128,3584]{1,0:T(8,128)(2,1)} %tok_ref.1, s32[1,128]{1,0:T(1,128)} %bitcast.8, f32[1,128]{1,0:T(1,128)} %bitcast.9, bf16[1,3584]{1,0:T(2,128)(2,1)} %reshape.11.gain_ref, bf16[3584,128]{1,0:T(8,128)(2,1)} %bitcast.5, bf16[3584,128]{1,0:T(8,128)(2,1)} %bitcast.6, bf16[128,3584]{1,0:T(8,128)(2,1)} %bitcast.7), custom_call_target="tpu_custom_call" | custom-call | flops 6341787648 | bytes 8388608 | tf_op jit(solution)/shard_map/pallas_call | solution.py:334
  90.2 2.2 %copy.9 = bf16[128,3584]{1,0:T(8,128)(2,1)} copy(bf16[128,3584]{1,0:T(8,128)(2,1)} %shard_map.73) | data formatting | bytes 1835008
Async XLA Ops:
  0.0 0.7 copy-start
